TPU v7x, 32 devices: a whole 2x2x4 slice. The times are simulated.
32 devices in a mesh: lat: 8 (over z, x), deg: 4 (over y, core).
Axes of the slice: x: 2, y: 2, z: 4, core: 2. Of those that a mesh axis runs over, the one named last changes fastest.
Arguments:
- eta_tl: float32 [64, 10752], P('lat'), may hold values from -6 to 6
- vel_tl: float32 [2, 64, 10752], P(None, 'lat'), may hold values from -6 to 6
- eta_adj: float32 [64, 10752], P('lat'), may hold values from -6 to 6
- vel_adj: float32 [2, 64, 10752], P(None, 'lat'), may hold values from -6 to 6
- depth: float32 [64, 10752], P('lat'), may hold values from 0.2 to 1
- drag: float32 [64, 10752], P('lat'), may hold values from 0.01 to 0.3
- ocean: int32 [64, 10752], P('lat'), may hold values 0 or 1
- basis: bfloat16 [1024, 64, 1024], P('lat', None, 'deg'), may hold values from -5 to 5
- love: float32 [1024], P('deg'), may hold values from 0.05 to 0.5
Outputs:
- eta_tl_out: float32 [64, 10752], P('lat')
- vel_tl_out: float32 [2, 64, 10752], P(None, 'lat')
- eta_adj_out: float32 [64, 10752], P('lat')
- vel_adj_out: float32 [2, 64, 10752], P(None, 'lat')
All inputs are finite; a program needn't handle non-finite values. No bound on the sum of `ocean` on one device may be relied on, other than what follows from the above.
Results may differ from a plain program's by a relative error of at most 0.02.
Values may be sent and summed in bfloat16 or wider, within the bound.
A program may use at most 320 MiB of HBM per device.

v0:
```python
import jax
import jax.numpy as jnp
import numpy as np
from jax import lax
from jax.sharding import PartitionSpec as P

STEPS = 2
LANES = 128
kappa_x = 0.3
kappa_y = 0.4


def passed_along(value, axis, by):
    length = lax.axis_size(axis)
    pairs = [(i, i + by) for i in range(length) if 0 <= i + by < length]
    return lax.ppermute(value, axis, pairs)


def circle(numerator, period):
    angles = 2.0 * np.pi * (numerator % period) / period
    return (np.cos(angles), np.sin(angles))


def fourier_tables(lon_count, order_total):
    major = lon_count // LANES
    blocks = -(-order_total // major)
    residues, lanes = (np.arange(major), np.arange(LANES))
    outer = np.stack(circle(residues[:, None] * residues[None, :], major))
    turn = np.stack(circle(residues[:, None] * lanes[None, :], lon_count))
    inner = np.stack(circle(np.arange(blocks)[:, None] * lanes[None, :], LANES))
    return (
        jnp.asarray(outer, jnp.bfloat16),
        jnp.asarray(turn, jnp.float32),
        jnp.asarray(inner, jnp.bfloat16),
    )


def order_factor(orders):
    return jnp.where(orders == 0, 1.0, 2.0).astype(jnp.bfloat16)


def analyse(stacked, analysis_weight, tables, order_count):
    outer, turn, inner = tables
    row_count = stacked.shape[1]
    lon_count = stacked.shape[2]
    split_rows = stacked.astype(jnp.bfloat16).reshape(2 * row_count, lon_count // LANES, LANES)
    first = jnp.einsum("cka,rab->crkb", outer, split_rows, preferred_element_type=jnp.float32)
    turned = jnp.stack(
        [first[0] * turn[0] - first[1] * turn[1], first[1] * turn[0] + first[0] * turn[1]]
    ).astype(jnp.bfloat16)
    second = jnp.stack([jnp.stack([inner[0], -inner[1]]), jnp.stack([inner[1], inner[0]])])
    spectra = jnp.einsum("crkb,dcnb->dnkr", turned, second, preferred_element_type=jnp.float32)
    spectra = spectra.reshape(2, -1, 2, row_count)[:, :order_count] * (1.0 / lon_count)
    return (spectra * analysis_weight[None, None, :, :]).astype(jnp.bfloat16)


def legendre(spectra, basis, love):
    coeffs = jnp.einsum("cmfi,mil->cmfl", spectra, basis, preferred_element_type=jnp.float32)
    scaled = (coeffs * love[None, None, None, :]).astype(jnp.bfloat16)
    return jnp.einsum("cmfl,mil->cmfi", scaled, basis, preferred_element_type=jnp.float32)


def synthesise(coeffs, factors, tables, output_weight):
    outer, turn, inner = tables
    major, blocks = (turn.shape[1], inner.shape[1])
    order_count = coeffs.shape[1]
    row_count = coeffs.shape[3]
    scaled = coeffs * factors[None, :, None, None]
    padded = jnp.pad(scaled, ((0, 0), (0, major * blocks - order_count), (0, 0), (0, 0)))
    padded = padded.reshape(2, blocks, major, 2 * row_count)
    second = jnp.stack([jnp.stack([inner[0], inner[1]]), jnp.stack([-inner[1], inner[0]])])
    first = jnp.einsum("cnkr,dcnb->drkb", padded, second, preferred_element_type=jnp.float32)
    turned = jnp.stack(
        [first[0] * turn[0] + first[1] * turn[1], first[1] * turn[0] - first[0] * turn[1]]
    ).astype(jnp.bfloat16)
    grid_out = jnp.einsum("cka,crkb->rab", outer, turned, preferred_element_type=jnp.float32)
    return grid_out.reshape(2, row_count, -1) * output_weight[:, :, None]


def edges_from(rows, by):
    sent = jnp.concatenate(rows, 0).astype(jnp.bfloat16)
    got = passed_along(sent, "lat", by).astype(jnp.float32)
    return [got[i : i + 1] for i in range(len(rows))]


def northward(values, edge):
    return jnp.concatenate([values[1:], edge], 0)


def southward(values, edge):
    return jnp.concatenate([edge, values[:-1]], 0)


def on_device(eta_tl, vel_tl, eta_adj, vel_adj, depth, drag, ocean, basis, love):
    row_count = eta_tl.shape[0]
    lon_count = eta_tl.shape[1]
    lat_count = lax.axis_size("lat")
    total_rows = row_count * lat_count
    first_row = lax.axis_index("lat") * row_count
    indices = first_row + jnp.arange(row_count, dtype=jnp.int32)
    latitude = (indices.astype(jnp.float32) + 0.5) * (jnp.pi / total_rows) - 0.5 * jnp.pi
    cosine = jnp.cos(latitude)
    quad_weight = jnp.pi / total_rows * cosine
    east_factor = (kappa_x / (0.5 + 0.5 * cosine))[:, None]
    wet_mask = ocean.astype(jnp.float32)
    flux_north = kappa_y * wet_mask * eta_adj
    north_depth, north_wet, north_flux = edges_from([depth[:1], wet_mask[:1], flux_north[:1]], -1)
    depth_up = northward(depth, north_depth)
    wet_up = northward(wet_mask, north_wet)
    mask_u = wet_mask * jnp.roll(wet_mask, -1, 1)
    mask_v = wet_mask * wet_up
    depth_u = 0.5 * (depth + jnp.roll(depth, -1, 1))
    depth_v = 0.5 * (depth + depth_up)
    retain = 1.0 - drag
    ones_weight = jnp.ones_like(quad_weight)
    analysis_weight = jnp.stack([quad_weight, ones_weight])
    output_weight = jnp.stack([ones_weight, quad_weight])
    owned_count = basis.shape[0]
    order_total = owned_count * lat_count
    full_orders = jnp.arange(order_total, dtype=jnp.int32)
    tables = fourier_tables(lon_count, order_total)
    full_factor = order_factor(full_orders)
    state_eta, state_vel = (eta_tl, vel_tl)
    back_eta, back_vel = (eta_adj, vel_adj)

    def adjoint_terms(eta, vel, flux_edge):
        flux_east = east_factor * wet_mask * eta
        flux_up = kappa_y * wet_mask * eta
        north_up = northward(flux_up, flux_edge)
        p_term = mask_u * (vel[0] + depth_u * (jnp.roll(flux_east, -1, 1) - flux_east))
        q_term = mask_v * (vel[1] + depth_v * (north_up - flux_up))
        return (p_term, q_term)

    p_term, q_term = adjoint_terms(back_eta, back_vel, north_flux)
    (q_edge,) = edges_from([q_term[-1:]], 1)
    for step_index in range(STEPS):
        flux_p = east_factor * p_term
        q_down = southward(q_term, q_edge)
        psi_bar = flux_p - jnp.roll(flux_p, 1, 1) + kappa_y * (q_term - q_down)
        spectra = analyse(jnp.stack([state_eta, psi_bar]), analysis_weight, tables, order_total)
        owned_rows = lax.all_to_all(spectra, "lat", split_axis=1, concat_axis=3, tiled=True)
        partial_value = legendre(owned_rows, basis, love)
        total_sum = lax.psum(partial_value.astype(jnp.bfloat16), "deg")
        banded = lax.all_to_all(total_sum, "lat", split_axis=3, concat_axis=1, tiled=True)
        loads = synthesise(banded, full_factor, tables, output_weight)
        last = step_index == STEPS - 1
        psi_now = state_eta - loads[0]
        back_eta = back_eta + psi_bar - loads[1]
        back_vel = (retain * p_term, retain * q_term)
        north_rows = [psi_now[:1]]
        if not last:
            north_rows.append(kappa_y * wet_mask[:1] * back_eta[:1])
        north_edges = edges_from(north_rows, -1)
        psi_up = northward(psi_now, north_edges[0])
        new_u = mask_u * (
            retain * state_vel[0] - east_factor * (jnp.roll(psi_now, -1, 1) - psi_now)
        )
        new_v = mask_v * (retain * state_vel[1] - kappa_y * (psi_up - psi_now))
        flux_x = depth_u * new_u
        flux_y = depth_v * new_v
        south_rows = [flux_y[-1:]]
        if not last:
            p_term, q_term = adjoint_terms(back_eta, back_vel, north_edges[1])
            south_rows.append(q_term[-1:])
        south_edges = edges_from(south_rows, 1)
        flux_down = southward(flux_y, south_edges[0])
        if not last:
            q_edge = south_edges[1]
        state_eta = state_eta - wet_mask * (
            east_factor * (flux_x - jnp.roll(flux_x, 1, 1)) + kappa_y * (flux_y - flux_down)
        )
        state_vel = (new_u, new_v)
    state_vel, back_vel = (jnp.stack(state_vel), jnp.stack(back_vel))
    return (state_eta, state_vel, back_eta, back_vel)


def solution(mesh):
    in_specs = (
        P("lat", None),
        P(None, "lat", None),
        P("lat", None),
        P(None, "lat", None),
        P("lat", None),
        P("lat", None),
        P("lat", None),
        P("lat", None, "deg"),
        P("deg"),
    )
    out_specs = (P("lat", None), P(None, "lat", None), P("lat", None), P(None, "lat", None))
    return jax.shard_map(
        on_device, mesh=mesh, in_specs=in_specs, out_specs=out_specs, check_vma=False
    )
```

profile of v0, /device:TPU:0, one launch (start us, length us, event | category | flops | bytes accessed | tf_op | source)
XLA Modules:
  0.0 200.0 jit_solution(16623130963314955521)
XLA Ops:
  7.3 1.0 slice.442
  8.3 1.0 convert_element_type.99
  9.3 1.3 multiply_multiply_fusion.3
  10.8 1.3 collective-permute-start
  12.8 0.5 copy-done.4
  13.4 4.8 %collective-permute-done = bf16[3,10752]{1,0:T(4,128)(2,1)S(1)} collective-permute-done((bf16[3,10752]{1,0:T(4,128)(2,1)S(1)}, bf16[3,10752]{1,0:T(4,128)(2,1)S(1)}, u32[]{:S(2)}, u32[]{:S(2)}) %collective-permute-start) | collective-permute-done | bytes 64544 | tf_op jit(solution)/shard_map/ppermute | solution.py:16
  18.3 1.3 broadcast_multiply_fusion.3
  19.7 4.8 %collective-permute-start.1 = (bf16[1,10752]{1,0:T(2,128)(2,1)S(1)}, bf16[1,10752]{1,0:T(2,128)(2,1)S(1)}, u32[]{:S(2)}, u32[]{:S(2)}) collective-permute-start(bf16[1,10752]{1,0:T(2,128)(2,1)S(1)} %slice.440), channel_id=1, source_target_pairs={{0,4},{4,8},{8,12},{12,16},{16,20},{20,24},{24,28},{1,5},{5,9},{9,... | collective-permute-start | bytes 64520 | tf_op jit(solution)/shard_map/ppermute | solution.py:16
  24.6 1.6 collective-permute-done.1
  26.2 0.9 convert_bitcast_fusion.2
  27.4 0.3 convolution_bitcast_fusion.3
  27.7 0.2 copy-done.19
  28.1 0.5 copy-done.33
  28.7 0.4 convolution_bitcast_fusion.7
  29.3 0.7 copy.57
  30.0 1.1 reshape.104
  31.1 12.4 %all_to_all.72 = bf16[8,2,2048]{2,1,0:T(2,128)(2,1)S(1)} all-to-all(bf16[8,2,2048]{2,1,0:T(2,128)(2,1)S(1)} %reshape.104), channel_id=1, replica_groups=mesh['lat'=8,'deg'=4] {'lat'}, dimensions={0} | all-to-all | bytes 131072 | tf_op jit(solution)/shard_map/all_to_all | solution.py:141
  43.5 1.2 reshape.105
  44.7 1.3 copy.90
  46.2 6.0 %fusion.45 = bf16[2,128,2,64]{3,2,0,1:T(2,128)(2,1)} fusion(bf16[128,64,256]{2,1,0:T(8,128)(2,1)} %param.19, bf16[2,128,2,64]{3,2,0,1:T(2,128)(2,1)S(1)} %copy.60, f32[256]{0:T(256)S(1)} %copy-done.31), kind=kOutput, calls=%fused_computation.25 | convolution fusion | flops 33849344 | bytes 4326400 | tf_op jit(solution)/shard_map/cmfl,mil->cmfi/dot_general | solution.py:60
  52.2 29.1 %all-reduce.7.cloned.1.call-done = bf16[2,128,2,64]{3,2,0,1:T(2,128)(2,1)} async-done(((bf16[2,128,2,64]{3,2,0,1:T(2,128)(2,1)}), bf16[2,128,2,64]{3,2,0,1:T(2,128)(2,1)}) %all-reduce.7.cloned.1.call-update) | async-done | bytes 65552 | tf_op jit(solution)/shard_map/psum | solution.py:143
  81.3 1.7 copy.61
  83.0 5.5 %all-to-all-start.1 = ((bf16[2,128,2,64]{1,2,0,3:T(2,128)(2,1)}), bf16[2,128,2,64]{1,2,0,3:T(2,128)(2,1)S(1)}, u32[]{:S(2)}, u32[]{:S(2)}) async-start(bf16[2,128,2,64]{1,2,0,3:T(2,128)(2,1)} %copy.61), calls=%async_computation.1 | async-start | bytes 131072 | tf_op jit(solution)/shard_map/all_to_all | solution.py:144
  88.5 6.8 %all-to-all-done.1 = bf16[2,128,2,64]{1,2,0,3:T(2,128)(2,1)S(1)} async-done(((bf16[2,128,2,64]{1,2,0,3:T(2,128)(2,1)}), bf16[2,128,2,64]{1,2,0,3:T(2,128)(2,1)S(1)}, u32[]{:S(2)}, u32[]{:S(2)}) %all-to-all-start.1) | async-done | bytes 65568 | tf_op jit(solution)/shard_map/all_to_all | solution.py:144
  95.4 0.2 reshape.79
  95.6 0.4 convolution_bitcast_fusion.2
  96.2 0.3 convolution_bitcast_fusion.5
  96.8 0.8 copy-done.12
  98.0 0.7 copy-done.2
  98.9 1.3 collective-permute-start.2
  100.2 0.9 multiply_bitcast_fusion.1
  101.4 3.5 %collective-permute-done.2 = bf16[2,10752]{1,0:T(2,128)(2,1)S(1)} collective-permute-done((bf16[2,10752]{1,0:T(2,128)(2,1)S(1)}, bf16[2,10752]{1,0:T(2,128)(2,1)S(1)}, u32[]{:S(2)}, u32[]{:S(2)}) %collective-permute-start.2) | collective-permute-done | bytes 43040 | tf_op jit(solution)/shard_map/ppermute | solution.py:16
  104.9 1.3 fusion.128
  106.5 3.4 %collective-permute-start.3 = (bf16[2,10752]{1,0:T(2,128)(2,1)S(1)}, bf16[2,10752]{1,0:T(2,128)(2,1)S(1)}, u32[]{:S(2)}, u32[]{:S(2)}) collective-permute-start(bf16[2,10752]{1,0:T(2,128)(2,1)S(1)} %pad_maximum_fusion.6), channel_id=1, source_target_pairs={{0,4},{4,8},{8,12},{12,16},{16,20},{20,24},{24,28},{1,5},{5,9},{9,... | collective-permute-start | bytes 129032 | tf_op jit(solution)/shard_map/ppermute | solution.py:16
  110.0 1.3 collective-permute-done.3
  111.4 0.2 convert_bitcast_fusion.1
  112.1 0.3 convolution_bitcast_fusion.1
  112.4 0.3 copy-done.21
  112.9 0.5 copy-done.34
  113.4 0.4 convolution_bitcast_fusion.6
  114.0 0.7 copy.66
  114.7 1.1 reshape.106
  115.8 10.6 %all_to_all.73 = bf16[8,2,2048]{2,1,0:T(2,128)(2,1)S(1)} all-to-all(bf16[8,2,2048]{2,1,0:T(2,128)(2,1)S(1)} %reshape.106), channel_id=1, replica_groups=mesh['lat'=8,'deg'=4] {'lat'}, dimensions={0} | all-to-all | bytes 131072 | tf_op jit(solution)/shard_map/all_to_all | solution.py:141
  126.4 1.2 reshape.107
  127.6 1.3 copy.96
  129.1 6.0 %fusion.40 = bf16[2,128,2,64]{3,2,0,1:T(2,128)(2,1)} fusion(bf16[128,64,256]{2,1,0:T(8,128)(2,1)} %param.19, bf16[2,128,2,64]{3,2,0,1:T(2,128)(2,1)S(1)} %copy.69, f32[256]{0:T(256)S(1)} %copy-done.32), kind=kOutput, calls=%fused_computation.24 | convolution fusion | flops 33849344 | bytes 4326400 | tf_op jit(solution)/shard_map/cmfl,mil->cmfi/dot_general | solution.py:60
  135.1 28.1 %all-reduce.9.cloned.1.call-done = bf16[2,128,2,64]{3,2,0,1:T(2,128)(2,1)} async-done(((bf16[2,128,2,64]{3,2,0,1:T(2,128)(2,1)}), bf16[2,128,2,64]{3,2,0,1:T(2,128)(2,1)}) %all-reduce.9.cloned.1.call-update) | async-done | bytes 65552 | tf_op jit(solution)/shard_map/psum | solution.py:143
  163.2 1.0 copy.70
  164.3 12.2 %all_to_all.74 = bf16[2,128,2,64]{1,2,0,3:T(2,128)(2,1)S(1)} all-to-all(bf16[2,128,2,64]{1,2,0,3:T(2,128)(2,1)S(1)} %copy.70), channel_id=1, replica_groups=mesh['lat'=8,'deg'=4] {'lat'}, dimensions={3} | all-to-all | bytes 131072 | tf_op jit(solution)/shard_map/all_to_all | solution.py:144
  176.5 0.2 reshape.82
  176.7 0.4 convolution_bitcast_fusion
  177.2 0.2 add_convert_fusion
  177.4 0.3 convolution_bitcast_fusion.4
  177.7 1.0 reshape.83
  178.6 1.2 broadcast_multiply_fusion
  179.9 0.8 fusion.62
  180.8 1.4 collective-permute-start.4
  182.2 0.9 pad_maximum_fusion.1
  183.3 3.5 %collective-permute-done.4 = bf16[1,10752]{1,0:T(2,128)(2,1)S(1)} collective-permute-done((bf16[1,10752]{1,0:T(2,128)(2,1)S(1)}, bf16[1,10752]{1,0:T(2,128)(2,1)S(1)}, u32[]{:S(2)}, u32[]{:S(2)}) %collective-permute-start.4) | collective-permute-done | bytes 21536 | tf_op jit(solution)/shard_map/ppermute | solution.py:16
  186.9 0.3 fusion.119
  187.3 3.2 %collective-permute-start.5 = (bf16[1,10752]{1,0:T(2,128)(2,1)S(1)}, bf16[1,10752]{1,0:T(2,128)(2,1)S(1)}, u32[]{:S(2)}, u32[]{:S(2)}) collective-permute-start(bf16[1,10752]{1,0:T(2,128)(2,1)S(1)} %slice.435), channel_id=1, source_target_pairs={{0,4},{4,8},{8,12},{12,16},{16,20},{20,24},{24,28},{1,5},{5,9},{9,... | collective-permute-start | bytes 64520 | tf_op jit(solution)/shard_map/ppermute | solution.py:16
  190.5 0.9 pad_maximum_fusion
  191.4 0.7 collective-permute-done.5
  192.2 0.9 fusion.101
  (135 shorter events, 5.2 us)
Async XLA Ops:
  7.2 74.1 %all-reduce.7.cloned.1.call-start = ((), (), s32[]{:S(2)}) async-start(), calls=%async_computation.4 | async-start | bytes 262144 | tf_op jit(solution)/shard_map/psum | solution.py:143
  9.3 3.1 %copy-start.1 = (f32[8,10752]{1,0:T(8,128)}, f32[8,10752]{1,0:T(8,128)S(1)}, u32[]{:S(2)}) copy-start(f32[8,10752]{1,0:T(8,128)S(1)} %convert_element_type.99) | copy-start | bytes 1032196
  9.3 3.0 %copy-start.3 = (f32[8,10752]{1,0:T(8,128)S(1)}, f32[8,10752]{1,0:T(8,128)}, u32[]{:S(2)}) copy-start(f32[8,10752]{1,0:T(8,128)} %param.16) | copy-start | bytes 1032196
  10.8 7.4 %collective-permute-start = (bf16[3,10752]{1,0:T(4,128)(2,1)S(1)}, bf16[3,10752]{1,0:T(4,128)(2,1)S(1)}, u32[]{:S(2)}, u32[]{:S(2)}) collective-permute-start(bf16[3,10752]{1,0:T(4,128)(2,1)S(1)} %pad_maximum_fusion.4), channel_id=1, source_target_pairs={{4,0},{8,4},{12,8},{16,12},{20,16},{24,20},{28,24},{5,1},{9,5},{13... | collective-permute-start | bytes 193544 | tf_op jit(solution)/shard_map/ppermute | solution.py:16
  12.4 1.0 copy-start.4
  12.5 5.8 %copy-start = (s32[8,10752]{1,0:T(8,128)S(1)}, s32[8,10752]{1,0:T(8,128)}, u32[]{:S(2)}) copy-start(s32[8,10752]{1,0:T(8,128)} %param.18) | copy-start | bytes 1032196
  12.5 5.8 %slice-start = ((f32[8,10752]{1,0:T(8,128)}), f32[8,1]{1,0:T(8,128)S(1)}, s32[]{:S(2)}) async-start(f32[8,10752]{1,0:T(8,128)} %copy-done.1), calls=%async_computation.6 | async-start | bytes 8192 | tf_op jit(solution)/shard_map/jit(_roll_static)/slice | solution.py:110
  12.5 5.8 %slice-start.1 = ((f32[8,10752]{1,0:T(8,128)}), f32[8,1]{1,0:T(8,128)S(1)}, s32[]{:S(2)}) async-start(f32[8,10752]{1,0:T(8,128)} %param.16), calls=%async_computation.7 | async-start | bytes 8192 | tf_op jit(solution)/shard_map/jit(_roll_static)/slice | solution.py:112
  12.6 5.8 %copy-start.23 = (f32[2,8,10752]{2,1,0:T(8,128)S(1)}, f32[2,8,10752]{2,1,0:T(8,128)}, u32[]{:S(2)}) copy-start(f32[2,8,10752]{2,1,0:T(8,128)} %param.15) | copy-start | bytes 2064388
  19.7 6.4 %collective-permute-start.1 = (bf16[1,10752]{1,0:T(2,128)(2,1)S(1)}, bf16[1,10752]{1,0:T(2,128)(2,1)S(1)}, u32[]{:S(2)}, u32[]{:S(2)}) collective-permute-start(bf16[1,10752]{1,0:T(2,128)(2,1)S(1)} %slice.440), channel_id=1, source_target_pairs={{0,4},{4,8},{8,12},{12,16},{16,20},{20,24},{24,28},{1,5},{5,9},{9,... | collective-permute-start | bytes 64520 | tf_op jit(solution)/shard_map/ppermute | solution.py:16
  24.5 4.7 %copy-start.29 = (f32[2,8]{1,0:T(2,128)}, f32[2,8]{1,0:T(2,128)S(1)}, u32[]{:S(2)}) copy-start(f32[2,8]{1,0:T(2,128)S(1)} %get-tuple-element.62) | copy-start | bytes 196
  24.5 72.2 %copy-start.27 = (f32[2,8]{1,0:T(2,128)}, f32[2,8]{1,0:T(2,128)S(1)}, u32[]{:S(2)}) copy-start(f32[2,8]{1,0:T(2,128)S(1)} %get-tuple-element.61) | copy-start | bytes 196
  26.2 1.2 copy-start.18
  27.1 0.8 copy-start.19
  27.1 0.8 copy-start.20
  27.9 0.7 copy-start.33
  31.1 15.1 %copy-start.31 = (f32[256]{0:T(256)S(1)}, f32[256]{0:T(256)}, u32[]{:S(2)}) copy-start(f32[256]{0:T(256)} %param.20) | copy-start | bytes 3076
  46.1 49.5 %copy-start.25 = (bf16[2,2,13,128,1]{3,2,1,0,4:T(8,128)(2,1)S(1)}, bf16[2,2,13,128,1]{3,2,1,0,4:T(8,128)(2,1)}, u32[]{:S(2)}) copy-start(bf16[2,2,13,128,1]{3,2,1,0,4:T(8,128)(2,1)} %constant.67) | copy-start | bytes 39940
  83.0 12.4 %all-to-all-start.1 = ((bf16[2,128,2,64]{1,2,0,3:T(2,128)(2,1)}), bf16[2,128,2,64]{1,2,0,3:T(2,128)(2,1)S(1)}, u32[]{:S(2)}, u32[]{:S(2)}) async-start(bf16[2,128,2,64]{1,2,0,3:T(2,128)(2,1)} %copy.61), calls=%async_computation.1 | async-start | bytes 131072 | tf_op jit(solution)/shard_map/all_to_all | solution.py:144
  88.5 74.7 %all-reduce.9.cloned.1.call-start = ((), (), s32[]{:S(2)}) async-start(), calls=%async_computation.5 | async-start | bytes 262144 | tf_op jit(solution)/shard_map/psum | solution.py:143
  96.7 1.0 copy-start.12
  96.7 1.1 copy-start.13
  97.8 1.0 copy-start.2
  97.8 2.5 %copy-start.5 = (f32[8,10752]{1,0:T(8,128)S(1)}, f32[8,10752]{1,0:T(8,128)}, u32[]{:S(2)}) copy-start(f32[8,10752]{1,0:T(8,128)} %param.17) | copy-start | bytes 1032196
  97.8 2.5 %copy-start.17 = (f32[8,10752]{1,0:T(8,128)S(1)}, f32[8,10752]{1,0:T(8,128)}, u32[]{:S(2)}) copy-start(f32[8,10752]{1,0:T(8,128)} %get-tuple-element.28) | copy-start | bytes 1032196
  98.9 5.9 %collective-permute-start.2 = (bf16[2,10752]{1,0:T(2,128)(2,1)S(1)}, bf16[2,10752]{1,0:T(2,128)(2,1)S(1)}, u32[]{:S(2)}, u32[]{:S(2)}) collective-permute-start(bf16[2,10752]{1,0:T(2,128)(2,1)S(1)} %pad_maximum_fusion.5), channel_id=1, source_target_pairs={{4,0},{8,4},{12,8},{16,12},{20,16},{24,20},{28,24},{5,1},{9,5},{13... | collective-permute-start | bytes 129032 | tf_op jit(solution)/shard_map/ppermute | solution.py:16
  101.1 3.8 %copy-start.7 = (f32[8,10752]{1,0:T(8,128)S(1)}, f32[8,10752]{1,0:T(8,128)}, u32[]{:S(2)}) copy-start(f32[8,10752]{1,0:T(8,128)} %get-tuple-element.42) | copy-start | bytes 1032196
  101.1 3.8 %copy-start.9 = (f32[8,10752]{1,0:T(8,128)S(1)}, f32[8,10752]{1,0:T(8,128)}, u32[]{:S(2)}) copy-start(f32[8,10752]{1,0:T(8,128)} %get-tuple-element.43) | copy-start | bytes 1032196
  101.1 3.8 %copy-start.24 = (f32[2,8,10752]{2,1,0:T(8,128)S(1)}, f32[2,8,10752]{2,1,0:T(8,128)}, u32[]{:S(2)}) copy-start(f32[2,8,10752]{2,1,0:T(8,128)} %param.13) | copy-start | bytes 2064388
  106.5 4.9 %collective-permute-start.3 = (bf16[2,10752]{1,0:T(2,128)(2,1)S(1)}, bf16[2,10752]{1,0:T(2,128)(2,1)S(1)}, u32[]{:S(2)}, u32[]{:S(2)}) collective-permute-start(bf16[2,10752]{1,0:T(2,128)(2,1)S(1)} %pad_maximum_fusion.6), channel_id=1, source_target_pairs={{0,4},{4,8},{8,12},{12,16},{16,20},{20,24},{24,28},{1,5},{5,9},{9,... | collective-permute-start | bytes 129032 | tf_op jit(solution)/shard_map/ppermute | solution.py:16
  111.9 0.8 copy-start.21
  112.7 0.7 copy-start.34
  112.7 1.2 copy-start.30
  115.8 13.2 %copy-start.32 = (f32[256]{0:T(256)S(1)}, f32[256]{0:T(256)}, u32[]{:S(2)}) copy-start(f32[256]{0:T(256)} %param.20) | copy-start | bytes 3076
  129.0 47.7 %copy-start.26 = (bf16[2,2,13,128,1]{3,2,1,0,4:T(8,128)(2,1)S(1)}, bf16[2,2,13,128,1]{3,2,1,0,4:T(8,128)(2,1)}, u32[]{:S(2)}) copy-start(bf16[2,2,13,128,1]{3,2,1,0,4:T(8,128)(2,1)} %constant.67) | copy-start | bytes 39940
  135.1 42.1 %copy-start.22 = (f32[84,128]{1,0:T(8,128)S(1)}, f32[84,128]{1,0:T(8,128)}, u32[]{:S(2)}) copy-start(f32[84,128]{1,0:T(8,128)} %constant.64) | copy-start | bytes 129028
  177.4 1.3 copy-start.28
  179.8 2.4 %copy-start.11 = (f32[1,8,10752]{2,1,0:T(8,128)S(1)}, f32[1,8,10752]{2,1,0:T(8,128)}, u32[]{:S(2)}) copy-start(f32[1,8,10752]{2,1,0:T(8,128)} %get-tuple-element.44) | copy-start | bytes 1032196
  179.9 2.4 %copy-start.14 = (f32[1,8,10752]{2,1,0:T(8,128)S(1)}, f32[1,8,10752]{2,1,0:T(8,128)}, u32[]{:S(2)}) copy-start(f32[1,8,10752]{2,1,0:T(8,128)} %get-tuple-element.4) | copy-start | bytes 1032196
  180.7 6.2 %copy-start.6 = (f32[8,10752]{1,0:T(8,128)S(1)}, f32[8,10752]{1,0:T(8,128)}, u32[]{:S(2)}) copy-start(f32[8,10752]{1,0:T(8,128)} %param.17) | copy-start | bytes 1032196
  180.7 6.2 %copy-start.8 = (f32[8,10752]{1,0:T(8,128)S(1)}, f32[8,10752]{1,0:T(8,128)}, u32[]{:S(2)}) copy-start(f32[8,10752]{1,0:T(8,128)} %get-tuple-element.42) | copy-start | bytes 1032196
  180.7 6.2 %copy-start.10 = (f32[8,10752]{1,0:T(8,128)S(1)}, f32[8,10752]{1,0:T(8,128)}, u32[]{:S(2)}) copy-start(f32[8,10752]{1,0:T(8,128)} %get-tuple-element.43) | copy-start | bytes 1032196
  180.7 6.2 %copy-start.15 = (f32[8,10752]{1,0:T(8,128)S(1)}, f32[8,10752]{1,0:T(8,128)}, u32[]{:S(2)}) copy-start(f32[8,10752]{1,0:T(8,128)} %get-tuple-element.21) | copy-start | bytes 1032196
  180.7 6.2 %copy-start.16 = (f32[8,10752]{1,0:T(8,128)S(1)}, f32[8,10752]{1,0:T(8,128)}, u32[]{:S(2)}) copy-start(f32[8,10752]{1,0:T(8,128)} %get-tuple-element.40) | copy-start | bytes 1032196
  180.8 6.0 %collective-permute-start.4 = (bf16[1,10752]{1,0:T(2,128)(2,1)S(1)}, bf16[1,10752]{1,0:T(2,128)(2,1)S(1)}, u32[]{:S(2)}, u32[]{:S(2)}) collective-permute-start(bf16[1,10752]{1,0:T(2,128)(2,1)S(1)} %slice.436), channel_id=1, source_target_pairs={{4,0},{8,4},{12,8},{16,12},{20,16},{24,20},{28,24},{5,1},{9,5},{13... | collective-permute-start | bytes 64520 | tf_op jit(solution)/shard_map/ppermute | solution.py:16
  187.3 4.9 %collective-permute-start.5 = (bf16[1,10752]{1,0:T(2,128)(2,1)S(1)}, bf16[1,10752]{1,0:T(2,128)(2,1)S(1)}, u32[]{:S(2)}, u32[]{:S(2)}) collective-permute-start(bf16[1,10752]{1,0:T(2,128)(2,1)S(1)} %slice.435), channel_id=1, source_target_pairs={{0,4},{4,8},{8,12},{12,16},{16,20},{20,24},{24,28},{1,5},{5,9},{9,... | collective-permute-start | bytes 64520 | tf_op jit(solution)/shard_map/ppermute | solution.py:16
Sparse Core Ops, SparseCore 0:
  52.3 28.9 all-reduce.6
  135.2 27.9 all-reduce.8
where the time goes:
time: 201 us; the launch traced here: 200 us
  waiting for transfers between devices  79.5 us (40%)
  blocking collectives  35.2 us (18%)
  starting transfers between devices  20.9 us (10%)
  local copies, waits for them, and re-layouts  20.4 us (10%)
  between operations  15 us (7%)
  matrix products  14.8 us (7%)
  other arithmetic  14.2 us (7%)
    psum x2, waiting for transfers between devices, on_device(): total_sum = lax.psum(partial_value.astype(jnp.bfloat16), 'deg')  57.2 us
    all_to_all x2, blocking collectives, on_device(): lax.all_to_all(spectra, 'lat', split_axis=1, concat_axis=3, tiled=True)  23 us
    ppermute x6, waiting for transfers between devices, passed_along(): return lax.ppermute(value, axis, pairs)  15.4 us
    ppermute x6, starting transfers between devices, passed_along(): return lax.ppermute(value, axis, pairs)  15.3 us
    all_to_all x1, blocking collectives, on_device(): lax.all_to_all(total_sum, 'lat', split_axis=3, concat_axis=1, tiled=True)  12.2 us
    dot_general x2, matrix products, legendre(): jnp.einsum('cmfl,mil->cmfi', scaled, basis, preferred_element_type=jnp.fl...  12 us
    unnamed x74, local copies, waits for them, and re-layouts  8.38 us
    all_to_all x1, waiting for transfers between devices, on_device(): lax.all_to_all(total_sum, 'lat', split_axis=3, concat_axis=1, tiled=True)  6.85 us
  transfers between devices with their start and end apart: 9, of which 9 were waited for; matrix products, arithmetic and copies ran while one was open for 2% of the time, Pallas kernels for 0%

commit v1 on v0

--- a/solution.py
+++ b/solution.py
@@ -8,6 +8,10 @@
 LANES = 128
 kappa_x = 0.3
 kappa_y = 0.4
+
+
+def return_all_sample_in(v0, axis_id):
+    return lax.all_gather(v0, axis_name=axis_id).sum(axis=0)
 
 
 def passed_along(value, axis, by):
@@ -140,7 +144,7 @@
         spectra = analyse(jnp.stack([state_eta, psi_bar]), analysis_weight, tables, order_total)
         owned_rows = lax.all_to_all(spectra, "lat", split_axis=1, concat_axis=3, tiled=True)
         partial_value = legendre(owned_rows, basis, love)
-        total_sum = lax.psum(partial_value.astype(jnp.bfloat16), "deg")
+        total_sum = return_all_sample_in(partial_value.astype(jnp.bfloat16), "deg")
         banded = lax.all_to_all(total_sum, "lat", split_axis=3, concat_axis=1, tiled=True)
         loads = synthesise(banded, full_factor, tables, output_weight)
         last = step_index == STEPS - 1

time: 201 us -> 139 us (0.69)
  waiting for transfers between devices: 79.5 us -> 22.3 us
  between operations: 15 us -> 1.57 us
  blocking collectives: 35.2 us -> 46.5 us
  other arithmetic: 14.2 us -> 16.5 us
  starting transfers between devices: 20.9 us -> 18.7 us
    psum x2 -> x0, waiting for transfers between devices: 57.2 us -> none  [on_device(): total_sum = lax.psum(partial_value.astype(jnp.bfloat16), 'deg')]
    all_gather x0 -> x2, blocking collectives: none -> 14.2 us  [return_all_sample_in(): return lax.all_gather(v0, axis_name=axis_id).sum(axis=0)]
    all_to_all x1, blocking collectives: 12.2 us -> 9.3 us  [on_device(): lax.all_to_all(total_sum, 'lat', split_axis=3, concat_axis=1, tiled=True)]
    psum x2 -> x0, local copies, waits for them, and re-layouts: 2.7 us -> none  [on_device(): total_sum = lax.psum(partial_value.astype(jnp.bfloat16), 'deg')]
    reduce_sum x0 -> x2, other arithmetic: none -> 2.33 us  [return_all_sample_in(): return lax.all_gather(v0, axis_name=axis_id).sum(axis=0)]
    all_to_all x1, starting transfers between devices: 5.51 us -> 3.35 us  [on_device(): lax.all_to_all(total_sum, 'lat', split_axis=3, concat_axis=1, tiled=True)]
  transfers between devices with their start and end apart: 9 -> 7, of which waited for: 9 -> 7; matrix products, arithmetic and copies ran while one was open for 2% -> 3% of each run, Pallas kernels for 0% -> 0%
where the time goes in v1:
time: 139 us; the launch traced here: 138 us
  blocking collectives  46.5 us (33%)
  waiting for transfers between devices  22.3 us (16%)
  starting transfers between devices  18.7 us (13%)
  local copies, waits for them, and re-layouts  18.5 us (13%)
  other arithmetic  16.5 us (12%)
  matrix products  13.4 us (10%)
  between operations  1.57 us (1%)
    all_to_all x2, blocking collectives, on_device(): lax.all_to_all(spectra, 'lat', split_axis=1, concat_axis=3, tiled=True)  23 us
    ppermute x6, waiting for transfers between devices, passed_along(): return lax.ppermute(value, axis, pairs)  15.4 us
    ppermute x6, starting transfers between devices, passed_along(): return lax.ppermute(value, axis, pairs)  15.3 us
    all_gather x2, blocking collectives, return_all_sample_in(): return lax.all_gather(v0, axis_name=axis_id).sum(axis=0)  14.2 us
    dot_general x2, matrix products, legendre(): jnp.einsum('cmfl,mil->cmfi', scaled, basis, preferred_element_type=jnp.fl...  10.7 us
    all_to_all x1, blocking collectives, on_device(): lax.all_to_all(total_sum, 'lat', split_axis=3, concat_axis=1, tiled=True)  9.3 us
    unnamed x74, local copies, waits for them, and re-layouts  8.37 us
    all_to_all x1, waiting for transfers between devices, on_device(): lax.all_to_all(total_sum, 'lat', split_axis=3, concat_axis=1, tiled=True)  6.84 us
  transfers between devices with their start and end apart: 7, of which 7 were waited for; matrix products, arithmetic and copies ran while one was open for 3% of the time, Pallas kernels for 0%

profile of v1, /device:TPU:0, one launch (start us, length us, event | category | flops | bytes accessed | tf_op | source)
XLA Modules:
  0.0 137.5 jit_solution(17851817716444820063)
XLA Ops:
  0.7 1.0 slice.442
  1.7 1.0 convert_element_type.103
  2.8 1.3 multiply_multiply_fusion.3
  4.3 1.3 collective-permute-start
  6.2 0.5 copy-done.4
  6.8 4.8 %collective-permute-done = bf16[3,10752]{1,0:T(4,128)(2,1)S(1)} collective-permute-done((bf16[3,10752]{1,0:T(4,128)(2,1)S(1)}, bf16[3,10752]{1,0:T(4,128)(2,1)S(1)}, u32[]{:S(2)}, u32[]{:S(2)}) %collective-permute-start) | collective-permute-done | bytes 64544 | tf_op jit(solution)/shard_map/ppermute | solution.py:20
  11.8 1.3 broadcast_multiply_fusion.3
  13.1 4.8 %collective-permute-start.1 = (bf16[1,10752]{1,0:T(2,128)(2,1)S(1)}, bf16[1,10752]{1,0:T(2,128)(2,1)S(1)}, u32[]{:S(2)}, u32[]{:S(2)}) collective-permute-start(bf16[1,10752]{1,0:T(2,128)(2,1)S(1)} %slice.440), channel_id=1, source_target_pairs={{0,4},{4,8},{8,12},{12,16},{16,20},{20,24},{24,28},{1,5},{5,9},{9,... | collective-permute-start | bytes 64520 | tf_op jit(solution)/shard_map/ppermute | solution.py:20
  18.0 1.6 %collective-permute-done.1 = bf16[1,10752]{1,0:T(2,128)(2,1)S(1)} collective-permute-done((bf16[1,10752]{1,0:T(2,128)(2,1)S(1)}, bf16[1,10752]{1,0:T(2,128)(2,1)S(1)}, u32[]{:S(2)}, u32[]{:S(2)}) %collective-permute-start.1) | collective-permute-done | bytes 21536 | tf_op jit(solution)/shard_map/ppermute | solution.py:20
  19.6 0.9 convert_bitcast_fusion.2
  20.8 0.3 convolution_bitcast_fusion.3
  21.1 0.2 copy-done.19
  21.6 0.5 copy-done.33
  22.1 0.4 convolution_bitcast_fusion.7
  22.7 0.7 copy.54
  23.4 1.1 reshape.106
  24.5 12.4 %all_to_all.72 = bf16[8,2,2048]{2,1,0:T(2,128)(2,1)S(1)} all-to-all(bf16[8,2,2048]{2,1,0:T(2,128)(2,1)S(1)} %reshape.106), channel_id=1, replica_groups=mesh['lat'=8,'deg'=4] {'lat'}, dimensions={0} | all-to-all | bytes 131072 | tf_op jit(solution)/shard_map/all_to_all | solution.py:145
  36.9 1.2 reshape.107
  38.1 1.3 copy.87
  39.6 5.3 %fusion.45 = bf16[2,128,2,64]{3,2,0,1:T(2,128)(2,1)S(1)} fusion(bf16[128,64,256]{2,1,0:T(8,128)(2,1)} %param.19, bf16[2,128,2,64]{3,2,0,1:T(2,128)(2,1)S(1)} %copy.57, f32[256]{0:T(256)S(1)} %copy-done.31), kind=kOutput, calls=%fused_computation.25 | convolution fusion | flops 33849344 | bytes 4326400 | tf_op jit(solution)/shard_map/cmfl,mil->cmfi/dot_general | solution.py:64
  44.9 7.5 %all-gather = bf16[8,128,2,64]{3,2,0,1:T(2,128)(2,1)S(1)} all-gather(bf16[2,128,2,64]{3,2,0,1:T(2,128)(2,1)S(1)} %fusion.45), channel_id=2, replica_groups=mesh['lat'=8,'deg'=4] {'deg'}, dimensions={0}, use_global_device_ids=true | all-gather | bytes 327680 | tf_op jit(solution)/shard_map/all_gather | solution.py:14
  52.4 1.2 reduce_sum.24
  53.5 0.7 copy.58
  54.3 3.3 %all-to-all-start.1 = ((bf16[2,128,2,64]{1,2,0,3:T(2,128)(2,1)}), bf16[2,128,2,64]{1,2,0,3:T(2,128)(2,1)S(1)}, u32[]{:S(2)}, u32[]{:S(2)}) async-start(bf16[2,128,2,64]{1,2,0,3:T(2,128)(2,1)} %copy.58), calls=%async_computation.1 | async-start | bytes 131072 | tf_op jit(solution)/shard_map/all_to_all | solution.py:148
  57.6 6.8 %all-to-all-done.1 = bf16[2,128,2,64]{1,2,0,3:T(2,128)(2,1)S(1)} async-done(((bf16[2,128,2,64]{1,2,0,3:T(2,128)(2,1)}), bf16[2,128,2,64]{1,2,0,3:T(2,128)(2,1)S(1)}, u32[]{:S(2)}, u32[]{:S(2)}) %all-to-all-start.1) | async-done | bytes 65568 | tf_op jit(solution)/shard_map/all_to_all | solution.py:148
  64.5 0.2 reshape.79
  64.7 0.4 convolution_bitcast_fusion.2
  65.3 0.3 convolution_bitcast_fusion.5
  65.9 0.8 copy-done.12
  67.1 0.7 copy-done.2
  68.0 1.3 collective-permute-start.2
  69.3 0.9 multiply_bitcast_fusion.1
  70.5 3.5 %collective-permute-done.2 = bf16[2,10752]{1,0:T(2,128)(2,1)S(1)} collective-permute-done((bf16[2,10752]{1,0:T(2,128)(2,1)S(1)}, bf16[2,10752]{1,0:T(2,128)(2,1)S(1)}, u32[]{:S(2)}, u32[]{:S(2)}) %collective-permute-start.2) | collective-permute-done | bytes 43040 | tf_op jit(solution)/shard_map/ppermute | solution.py:20
  74.0 1.3 fusion.128
  75.6 3.4 %collective-permute-start.3 = (bf16[2,10752]{1,0:T(2,128)(2,1)S(1)}, bf16[2,10752]{1,0:T(2,128)(2,1)S(1)}, u32[]{:S(2)}, u32[]{:S(2)}) collective-permute-start(bf16[2,10752]{1,0:T(2,128)(2,1)S(1)} %pad_maximum_fusion.6), channel_id=1, source_target_pairs={{0,4},{4,8},{8,12},{12,16},{16,20},{20,24},{24,28},{1,5},{5,9},{9,... | collective-permute-start | bytes 129032 | tf_op jit(solution)/shard_map/ppermute | solution.py:20
  79.1 1.3 collective-permute-done.3
  80.5 0.2 convert_bitcast_fusion.1
  81.2 0.3 convolution_bitcast_fusion.1
  81.5 0.3 copy-done.21
  82.0 0.5 copy-done.34
  82.5 0.4 convolution_bitcast_fusion.6
  83.1 0.7 copy.63
  83.8 1.1 reshape.108
  84.9 10.6 %all_to_all.73 = bf16[8,2,2048]{2,1,0:T(2,128)(2,1)S(1)} all-to-all(bf16[8,2,2048]{2,1,0:T(2,128)(2,1)S(1)} %reshape.108), channel_id=1, replica_groups=mesh['lat'=8,'deg'=4] {'lat'}, dimensions={0} | all-to-all | bytes 131072 | tf_op jit(solution)/shard_map/all_to_all | solution.py:145
  95.5 1.2 reshape.109
  96.7 1.3 copy.93
  98.2 5.3 %fusion.40 = bf16[2,128,2,64]{3,2,0,1:T(2,128)(2,1)S(1)} fusion(bf16[128,64,256]{2,1,0:T(8,128)(2,1)} %param.19, bf16[2,128,2,64]{3,2,0,1:T(2,128)(2,1)S(1)} %copy.66, f32[256]{0:T(256)S(1)} %copy-done.32), kind=kOutput, calls=%fused_computation.24 | convolution fusion | flops 33849344 | bytes 4326400 | tf_op jit(solution)/shard_map/cmfl,mil->cmfi/dot_general | solution.py:64
  103.5 6.8 %all-gather.1 = bf16[8,128,2,64]{3,2,0,1:T(2,128)(2,1)S(1)} all-gather(bf16[2,128,2,64]{3,2,0,1:T(2,128)(2,1)S(1)} %fusion.40), channel_id=3, replica_groups=mesh['lat'=8,'deg'=4] {'deg'}, dimensions={0}, use_global_device_ids=true | all-gather | bytes 327680 | tf_op jit(solution)/shard_map/all_gather | solution.py:14
  110.3 1.2 reduce_sum.25
  111.5 9.3 %all_to_all.74 = bf16[2,128,2,64]{1,2,0,3:T(2,128)(2,1)S(1)} all-to-all(bf16[2,128,2,64]{1,2,0,3:T(2,128)(2,1)S(1)} %copy.67), channel_id=1, replica_groups=mesh['lat'=8,'deg'=4] {'lat'}, dimensions={3} | all-to-all | bytes 131072 | tf_op jit(solution)/shard_map/all_to_all | solution.py:148
  120.9 0.2 reshape.82
  121.1 0.4 convolution_bitcast_fusion
  121.7 0.3 convolution_bitcast_fusion.4
  122.0 1.0 reshape.83
  123.0 1.2 broadcast_multiply_fusion
  124.2 0.8 fusion.62
  125.1 1.4 %collective-permute-start.4 = (bf16[1,10752]{1,0:T(2,128)(2,1)S(1)}, bf16[1,10752]{1,0:T(2,128)(2,1)S(1)}, u32[]{:S(2)}, u32[]{:S(2)}) collective-permute-start(bf16[1,10752]{1,0:T(2,128)(2,1)S(1)} %slice.436), channel_id=1, source_target_pairs={{4,0},{8,4},{12,8},{16,12},{20,16},{24,20},{28,24},{5,1},{9,5},{13... | collective-permute-start | bytes 64520 | tf_op jit(solution)/shard_map/ppermute | solution.py:20
  126.6 0.9 pad_maximum_fusion.1
  127.7 3.5 %collective-permute-done.4 = bf16[1,10752]{1,0:T(2,128)(2,1)S(1)} collective-permute-done((bf16[1,10752]{1,0:T(2,128)(2,1)S(1)}, bf16[1,10752]{1,0:T(2,128)(2,1)S(1)}, u32[]{:S(2)}, u32[]{:S(2)}) %collective-permute-start.4) | collective-permute-done | bytes 21536 | tf_op jit(solution)/shard_map/ppermute | solution.py:20
  131.3 0.3 fusion.119
  131.6 3.2 %collective-permute-start.5 = (bf16[1,10752]{1,0:T(2,128)(2,1)S(1)}, bf16[1,10752]{1,0:T(2,128)(2,1)S(1)}, u32[]{:S(2)}, u32[]{:S(2)}) collective-permute-start(bf16[1,10752]{1,0:T(2,128)(2,1)S(1)} %slice.435), channel_id=1, source_target_pairs={{0,4},{4,8},{8,12},{12,16},{16,20},{20,24},{24,28},{1,5},{5,9},{9,... | collective-permute-start | bytes 64520 | tf_op jit(solution)/shard_map/ppermute | solution.py:20
  134.8 0.9 pad_maximum_fusion
  135.8 0.7 collective-permute-done.5
  136.6 0.9 fusion.101
  (133 shorter events, 5.4 us)
Async XLA Ops:
  2.7 3.1 %copy-start.1 = (f32[8,10752]{1,0:T(8,128)}, f32[8,10752]{1,0:T(8,128)S(1)}, u32[]{:S(2)}) copy-start(f32[8,10752]{1,0:T(8,128)S(1)} %convert_element_type.103) | copy-start | bytes 1032196
  2.8 3.0 %copy-start.3 = (f32[8,10752]{1,0:T(8,128)S(1)}, f32[8,10752]{1,0:T(8,128)}, u32[]{:S(2)}) copy-start(f32[8,10752]{1,0:T(8,128)} %param.16) | copy-start | bytes 1032196
  4.3 7.4 %collective-permute-start = (bf16[3,10752]{1,0:T(4,128)(2,1)S(1)}, bf16[3,10752]{1,0:T(4,128)(2,1)S(1)}, u32[]{:S(2)}, u32[]{:S(2)}) collective-permute-start(bf16[3,10752]{1,0:T(4,128)(2,1)S(1)} %pad_maximum_fusion.4), channel_id=1, source_target_pairs={{4,0},{8,4},{12,8},{16,12},{20,16},{24,20},{28,24},{5,1},{9,5},{13... | collective-permute-start | bytes 193544 | tf_op jit(solution)/shard_map/ppermute | solution.py:20
  5.8 1.0 copy-start.4
  5.9 5.8 %copy-start = (s32[8,10752]{1,0:T(8,128)S(1)}, s32[8,10752]{1,0:T(8,128)}, u32[]{:S(2)}) copy-start(s32[8,10752]{1,0:T(8,128)} %param.18) | copy-start | bytes 1032196
  6.0 5.8 %slice-start = ((f32[8,10752]{1,0:T(8,128)}), f32[8,1]{1,0:T(8,128)S(1)}, s32[]{:S(2)}) async-start(f32[8,10752]{1,0:T(8,128)} %copy-done.1), calls=%async_computation.4 | async-start | bytes 8192 | tf_op jit(solution)/shard_map/jit(_roll_static)/slice | solution.py:114
  6.0 5.8 %slice-start.1 = ((f32[8,10752]{1,0:T(8,128)}), f32[8,1]{1,0:T(8,128)S(1)}, s32[]{:S(2)}) async-start(f32[8,10752]{1,0:T(8,128)} %param.16), calls=%async_computation.5 | async-start | bytes 8192 | tf_op jit(solution)/shard_map/jit(_roll_static)/slice | solution.py:116
  6.0 5.8 %copy-start.23 = (f32[2,8,10752]{2,1,0:T(8,128)S(1)}, f32[2,8,10752]{2,1,0:T(8,128)}, u32[]{:S(2)}) copy-start(f32[2,8,10752]{2,1,0:T(8,128)} %param.15) | copy-start | bytes 2064388
  13.1 6.4 %collective-permute-start.1 = (bf16[1,10752]{1,0:T(2,128)(2,1)S(1)}, bf16[1,10752]{1,0:T(2,128)(2,1)S(1)}, u32[]{:S(2)}, u32[]{:S(2)}) collective-permute-start(bf16[1,10752]{1,0:T(2,128)(2,1)S(1)} %slice.440), channel_id=1, source_target_pairs={{0,4},{4,8},{8,12},{12,16},{16,20},{20,24},{24,28},{1,5},{5,9},{9,... | collective-permute-start | bytes 64520 | tf_op jit(solution)/shard_map/ppermute | solution.py:20
  17.9 4.7 %copy-start.29 = (f32[2,8]{1,0:T(2,128)}, f32[2,8]{1,0:T(2,128)S(1)}, u32[]{:S(2)}) copy-start(f32[2,8]{1,0:T(2,128)S(1)} %get-tuple-element.62) | copy-start | bytes 196
  17.9 47.9 %copy-start.27 = (f32[2,8]{1,0:T(2,128)}, f32[2,8]{1,0:T(2,128)S(1)}, u32[]{:S(2)}) copy-start(f32[2,8]{1,0:T(2,128)S(1)} %get-tuple-element.61) | copy-start | bytes 196
  19.6 1.2 copy-start.18
  20.5 0.8 copy-start.19
  20.6 0.8 copy-start.20
  21.4 0.7 copy-start.33
  24.5 15.1 %copy-start.31 = (f32[256]{0:T(256)S(1)}, f32[256]{0:T(256)}, u32[]{:S(2)}) copy-start(f32[256]{0:T(256)} %param.20) | copy-start | bytes 3076
  44.9 19.8 %copy-start.25 = (bf16[2,2,13,128,1]{3,2,1,0,4:T(8,128)(2,1)S(1)}, bf16[2,2,13,128,1]{3,2,1,0,4:T(8,128)(2,1)}, u32[]{:S(2)}) copy-start(bf16[2,2,13,128,1]{3,2,1,0,4:T(8,128)(2,1)} %constant.70) | copy-start | bytes 39940
  54.3 10.2 %all-to-all-start.1 = ((bf16[2,128,2,64]{1,2,0,3:T(2,128)(2,1)}), bf16[2,128,2,64]{1,2,0,3:T(2,128)(2,1)S(1)}, u32[]{:S(2)}, u32[]{:S(2)}) async-start(bf16[2,128,2,64]{1,2,0,3:T(2,128)(2,1)} %copy.58), calls=%async_computation.1 | async-start | bytes 131072 | tf_op jit(solution)/shard_map/all_to_all | solution.py:148
  65.8 1.0 copy-start.12
  65.8 1.1 copy-start.13
  66.8 1.0 copy-start.2
  66.8 2.5 %copy-start.5 = (f32[8,10752]{1,0:T(8,128)S(1)}, f32[8,10752]{1,0:T(8,128)}, u32[]{:S(2)}) copy-start(f32[8,10752]{1,0:T(8,128)} %param.17) | copy-start | bytes 1032196
  66.9 2.5 %copy-start.17 = (f32[8,10752]{1,0:T(8,128)S(1)}, f32[8,10752]{1,0:T(8,128)}, u32[]{:S(2)}) copy-start(f32[8,10752]{1,0:T(8,128)} %get-tuple-element.28) | copy-start | bytes 1032196
  68.0 5.9 %collective-permute-start.2 = (bf16[2,10752]{1,0:T(2,128)(2,1)S(1)}, bf16[2,10752]{1,0:T(2,128)(2,1)S(1)}, u32[]{:S(2)}, u32[]{:S(2)}) collective-permute-start(bf16[2,10752]{1,0:T(2,128)(2,1)S(1)} %pad_maximum_fusion.5), channel_id=1, source_target_pairs={{4,0},{8,4},{12,8},{16,12},{20,16},{24,20},{28,24},{5,1},{9,5},{13... | collective-permute-start | bytes 129032 | tf_op jit(solution)/shard_map/ppermute | solution.py:20
  70.2 3.8 %copy-start.7 = (f32[8,10752]{1,0:T(8,128)S(1)}, f32[8,10752]{1,0:T(8,128)}, u32[]{:S(2)}) copy-start(f32[8,10752]{1,0:T(8,128)} %get-tuple-element.42) | copy-start | bytes 1032196
  70.2 3.8 %copy-start.9 = (f32[8,10752]{1,0:T(8,128)S(1)}, f32[8,10752]{1,0:T(8,128)}, u32[]{:S(2)}) copy-start(f32[8,10752]{1,0:T(8,128)} %get-tuple-element.43) | copy-start | bytes 1032196
  70.2 3.8 %copy-start.24 = (f32[2,8,10752]{2,1,0:T(8,128)S(1)}, f32[2,8,10752]{2,1,0:T(8,128)}, u32[]{:S(2)}) copy-start(f32[2,8,10752]{2,1,0:T(8,128)} %param.13) | copy-start | bytes 2064388
  75.6 4.9 %collective-permute-start.3 = (bf16[2,10752]{1,0:T(2,128)(2,1)S(1)}, bf16[2,10752]{1,0:T(2,128)(2,1)S(1)}, u32[]{:S(2)}, u32[]{:S(2)}) collective-permute-start(bf16[2,10752]{1,0:T(2,128)(2,1)S(1)} %pad_maximum_fusion.6), channel_id=1, source_target_pairs={{0,4},{4,8},{8,12},{12,16},{16,20},{20,24},{24,28},{1,5},{5,9},{9,... | collective-permute-start | bytes 129032 | tf_op jit(solution)/shard_map/ppermute | solution.py:20
  81.0 0.8 copy-start.21
  81.8 0.7 copy-start.34
  81.8 1.2 copy-start.30
  84.9 13.2 %copy-start.32 = (f32[256]{0:T(256)S(1)}, f32[256]{0:T(256)}, u32[]{:S(2)}) copy-start(f32[256]{0:T(256)} %param.20) | copy-start | bytes 3076
  103.5 17.6 %copy-start.26 = (bf16[2,2,13,128,1]{3,2,1,0,4:T(8,128)(2,1)S(1)}, bf16[2,2,13,128,1]{3,2,1,0,4:T(8,128)(2,1)}, u32[]{:S(2)}) copy-start(bf16[2,2,13,128,1]{3,2,1,0,4:T(8,128)(2,1)} %constant.70) | copy-start | bytes 39940
  110.3 11.2 %copy-start.22 = (f32[84,128]{1,0:T(8,128)S(1)}, f32[84,128]{1,0:T(8,128)}, u32[]{:S(2)}) copy-start(f32[84,128]{1,0:T(8,128)} %constant.67) | copy-start | bytes 129028
  121.7 1.3 copy-start.28
  124.2 2.4 %copy-start.11 = (f32[1,8,10752]{2,1,0:T(8,128)S(1)}, f32[1,8,10752]{2,1,0:T(8,128)}, u32[]{:S(2)}) copy-start(f32[1,8,10752]{2,1,0:T(8,128)} %get-tuple-element.44) | copy-start | bytes 1032196
  124.2 2.4 %copy-start.14 = (f32[1,8,10752]{2,1,0:T(8,128)S(1)}, f32[1,8,10752]{2,1,0:T(8,128)}, u32[]{:S(2)}) copy-start(f32[1,8,10752]{2,1,0:T(8,128)} %get-tuple-element.4) | copy-start | bytes 1032196
  125.1 6.2 %copy-start.6 = (f32[8,10752]{1,0:T(8,128)S(1)}, f32[8,10752]{1,0:T(8,128)}, u32[]{:S(2)}) copy-start(f32[8,10752]{1,0:T(8,128)} %param.17) | copy-start | bytes 1032196
  125.1 6.2 %copy-start.8 = (f32[8,10752]{1,0:T(8,128)S(1)}, f32[8,10752]{1,0:T(8,128)}, u32[]{:S(2)}) copy-start(f32[8,10752]{1,0:T(8,128)} %get-tuple-element.42) | copy-start | bytes 1032196
  125.1 6.2 %copy-start.10 = (f32[8,10752]{1,0:T(8,128)S(1)}, f32[8,10752]{1,0:T(8,128)}, u32[]{:S(2)}) copy-start(f32[8,10752]{1,0:T(8,128)} %get-tuple-element.43) | copy-start | bytes 1032196
  125.1 6.2 %copy-start.15 = (f32[8,10752]{1,0:T(8,128)S(1)}, f32[8,10752]{1,0:T(8,128)}, u32[]{:S(2)}) copy-start(f32[8,10752]{1,0:T(8,128)} %get-tuple-element.21) | copy-start | bytes 1032196
  125.1 6.2 %copy-start.16 = (f32[8,10752]{1,0:T(8,128)S(1)}, f32[8,10752]{1,0:T(8,128)}, u32[]{:S(2)}) copy-start(f32[8,10752]{1,0:T(8,128)} %get-tuple-element.40) | copy-start | bytes 1032196
  125.1 6.0 %collective-permute-start.4 = (bf16[1,10752]{1,0:T(2,128)(2,1)S(1)}, bf16[1,10752]{1,0:T(2,128)(2,1)S(1)}, u32[]{:S(2)}, u32[]{:S(2)}) collective-permute-start(bf16[1,10752]{1,0:T(2,128)(2,1)S(1)} %slice.436), channel_id=1, source_target_pairs={{4,0},{8,4},{12,8},{16,12},{20,16},{24,20},{28,24},{5,1},{9,5},{13... | collective-permute-start | bytes 64520 | tf_op jit(solution)/shard_map/ppermute | solution.py:20
  131.6 4.9 %collective-permute-start.5 = (bf16[1,10752]{1,0:T(2,128)(2,1)S(1)}, bf16[1,10752]{1,0:T(2,128)(2,1)S(1)}, u32[]{:S(2)}, u32[]{:S(2)}) collective-permute-start(bf16[1,10752]{1,0:T(2,128)(2,1)S(1)} %slice.435), channel_id=1, source_target_pairs={{0,4},{4,8},{8,12},{12,16},{16,20},{20,24},{24,28},{1,5},{5,9},{9,... | collective-permute-start | bytes 64520 | tf_op jit(solution)/shard_map/ppermute | solution.py:20
